TPU v7x, 256 devices: a whole 4x4x8 slice. The times are simulated.
256 devices in a mesh: member: 8 (over x, core), space: 32 (over y, z).
Axes of the slice: x: 4, y: 4, z: 8, core: 2. Of those that a mesh axis runs over, the one named last changes fastest.
Arguments:
- inputs: bfloat16 [16, 16384, 1024], P('member', 'space'), may hold values from -12 to 12
- weight_in: bfloat16 [1024, 1024], replicated, may hold values from -0.1875 to 0.1875
- bias_in: float32 [1024], replicated, may hold values from -3 to 3
- weight_out: bfloat16 [8, 1024], replicated, may hold values from -0.75 to 0.75
- bias_out: float32 [8], replicated, may hold values from -4 to 4
- target_field: float32 [8, 16384], P(None, 'space'), may hold values from -10 to 10
- variable_weight: float32 [8], replicated, may hold values from 4 to 40
Outputs:
- grad_inputs: bfloat16 [16, 16384, 1024], P('member', 'space')
- grad_weight_in: float32 [1024, 1024], P(('member', 'space'))
- grad_bias_in: float32 [1024], P(('member', 'space'))
- grad_weight_out: float32 [8, 1024], replicated
- grad_bias_out: float32 [8], replicated
All inputs are finite; a program needn't handle non-finite values.
Results may differ from a plain program's by a relative error of at most 0.005.
The roundings to bfloat16 on the way count: a program that leaves them out, or rounds other values in their place, can miss the bound.
Values sent between devices are 32-bit elements; how exact they have to be, the bound alone decides.
A program may use at most 64 MiB of HBM per device.

v0:
```python
import jax
import jax.numpy as jnp
from jax import lax
from jax.sharding import PartitionSpec as P

ALPHA = 0.95
DELTA_SQ = 0.0025
INV_ROOT2 = 0.7071067811865476
INV_ROOT2PI = 0.3989422804014327


def pair_grad(local_rows, members_all, target_rows, variable_weight):
    total = members_all.shape[0]
    epsilon_share = (1.0 - ALPHA) / total
    differ = local_rows[:, None] - members_all[None]
    spread = jnp.sum(differ / jnp.sqrt(differ * differ + DELTA_SQ), axis=1)
    missed = local_rows - target_rows[None]
    direct = missed / jnp.sqrt(missed * missed + DELTA_SQ)
    factor = (1.0 - epsilon_share) / (total * (total - 1))
    return variable_weight[None, :, None] * (direct / total - factor * spread)


def shards(inputs, weight_in, bias_in, weight_out, bias_out, target_field, variable_weight):
    mem_dev, cell_dev, width = inputs.shape
    num_vars = weight_out.shape[0]
    all_rows = inputs.reshape(mem_dev * cell_dev, width)
    preact = jnp.dot(all_rows, weight_in, preferred_element_type=jnp.float32) + bias_in[None]
    normal_cdf = 0.5 * (1.0 + lax.erf(preact * INV_ROOT2))
    active_b = (preact * normal_cdf).astype(jnp.bfloat16)
    outputs = lax.dot_general(
        weight_out, active_b, (((1,), (1,)), ((), ())), preferred_element_type=jnp.float32
    )
    outputs = outputs + bias_out[:, None]
    predicted = outputs.reshape(num_vars, mem_dev, cell_dev).transpose(1, 0, 2)
    everyone = lax.all_gather(predicted, "member", axis=0, tiled=True)
    gradient = pair_grad(predicted, everyone, target_field, variable_weight)
    grad_rows = gradient.transpose(1, 0, 2).reshape(num_vars, mem_dev * cell_dev)
    grad_bf = grad_rows.astype(jnp.bfloat16)
    back_active = lax.dot_general(
        grad_bf, weight_out, (((0,), (0,)), ((), ())), preferred_element_type=jnp.float32
    )
    slope = normal_cdf + preact * jnp.exp(-0.5 * preact * preact) * INV_ROOT2PI
    back_pre = (back_active * slope).astype(jnp.bfloat16)
    back_rows = lax.dot_general(
        back_pre, weight_in, (((1,), (1,)), ((), ())), preferred_element_type=jnp.float32
    )
    grad_inputs = back_rows.astype(jnp.bfloat16).reshape(mem_dev, cell_dev, width)
    weight_term = lax.dot_general(
        all_rows, back_pre, (((0,), (0,)), ((), ())), preferred_element_type=jnp.float32
    )
    bias_term = jnp.sum(back_pre.astype(jnp.float32), axis=0)
    grad_w_in, grad_b_in = (
        lax.psum_scatter(weight_term, ("member", "space"), scatter_dimension=0, tiled=True),
        lax.psum_scatter(bias_term, ("member", "space"), scatter_dimension=0, tiled=True),
    )
    out_term = jnp.dot(grad_bf, active_b, preferred_element_type=jnp.float32)
    out_bias = jnp.sum(grad_rows, axis=1)
    grad_w_out, grad_b_out = lax.psum((out_term, out_bias), ("member", "space"))
    return (grad_inputs, grad_w_in, grad_b_in, grad_w_out, grad_b_out)


def solution(mesh):
    placed = (P("member", "space", None), P(), P(), P(), P(), P(None, "space"), P())
    return jax.shard_map(
        shards,
        mesh=mesh,
        in_specs=placed,
        out_specs=(
            P("member", "space", None),
            P(("member", "space"), None),
            P(("member", "space")),
            P(),
            P(),
        ),
        check_vma=False,
    )
```

profile of v0, /device:TPU:2, one launch (start us, length us, event | category | flops | bytes accessed | tf_op | source)
XLA Modules:
  0.0 315.6 jit_solution(6029997728809652328)
XLA Ops:
  7.2 0.0 copy-start
  7.2 0.0 all-reduce.5.cloned.1.call-start
  7.2 1.5 copy-done
  8.8 0.0 copy-start.2
  8.8 0.0 copy-start.4
  8.8 0.0 copy-start.3
  8.8 0.0 copy-start.5
  8.8 0.0 copy-start.6
  8.8 4.2 %multiply_convert_fusion = (bf16[1024,1024]{1,0:T(8,128)(2,1)S(1)}, f32[1024,1024]{1,0:T(8,128)S(1)}) fusion(f32[1024]{0:T(1024)} %param.9, bf16[1024,1024]{1,0:T(8,128)(2,1)S(1)} %bitcast.29, bf16[1024,1024]{1,0:T(8,128)(2,1)} %param.8), kind=kOutput, calls=%fused_computation.8 | convolution fusion | flops 2153775104 | bytes 10489856 | tf_op jit(solution)/shard_map/dot_general | solution.py:27
  13.0 0.0 copy-start.1
  13.0 0.0 copy-done.2
  13.1 0.0 copy-done.4
  13.1 0.6 convolution_add_fusion
  13.7 12.9 %all_gather.3 = f32[16,8,512]{2,1,0:T(8,128)S(1)} all-gather(f32[2,8,512]{2,1,0:T(8,128)S(1)} %bitcast.31), channel_id=1, replica_groups=mesh['member'=8,'space'=32] {'member'}, dimensions={0}, use_global_device_ids=true | all-gather | bytes 294912 | tf_op jit(solution)/shard_map/all_gather | solution.py:35
  26.6 0.1 fusion.8
  26.7 0.0 copy-done.3
  26.7 0.0 copy-done.5
  26.8 0.2 fusion.10
  26.9 0.0 copy-done.6
  26.9 2.3 convert_reduce_fusion
  29.3 0.0 copy-done.1
  29.3 0.0 copy-start.7
  29.3 1.4 copy-done.7
  30.7 4.3 %convolution_bitcast_fusion = f32[1024,1024]{0,1:T(8,128)} fusion(bf16[1024,1024]{1,0:T(8,128)(2,1)S(1)} %get-tuple-element.28, bf16[1024,1024]{1,0:T(8,128)(2,1)S(1)} %bitcast.30), kind=kOutput, calls=%fused_computation.10 | convolution fusion | flops 2147483648 | bytes 8388608 | tf_op jit(solution)/shard_map/dot_general | solution.py:48
  35.0 0.0 all-reduce.5.cloned.1.call-update
  35.0 2.0 fusion.12
  37.0 79.8 %all-reduce.2 = (f32[1024]{0:T(1024)S(1)}, f32[8,1024]{1,0:T(8,128)}, f32[8]{0:T(128)}) all-reduce(f32[1024]{0:T(1024)S(1)} %get-tuple-element.27, f32[8,1024]{1,0:T(8,128)S(1)} %fusion.12, f32[8]{0:T(128)S(1)} %get-tuple-element.23), channel_id=3, replica_groups=mesh['member'=8,'space'=32] {'member','space'}, use_global_device_ids=true, to_apply=%region_3.0.clone | all-reduce | flops 9224 | bytes 73792
  116.8 0.6 dynamic-slice.1
  117.4 5.9 %convolution_convert_fusion = bf16[1024,1024]{1,0:T(8,128)(2,1)} fusion(bf16[1024,1024]{1,0:T(8,128)(2,1)} %copy-done.7, bf16[1024,1024]{1,0:T(8,128)(2,1)} %param.8), kind=kOutput, calls=%fused_computation.11 | convolution fusion | flops 2148532224 | bytes 6291456 | tf_op jit(solution)/shard_map/dot_general | solution.py:44
  123.3 183.4 %all-reduce.5.cloned.1.call-done = f32[1024,1024]{0,1:T(8,128)} async-done(((f32[1024,1024]{0,1:T(8,128)}), f32[1024,1024]{0,1:T(8,128)}) %all-reduce.5.cloned.1.call-update) | async-done | bytes 4194320
  306.7 1.2 constant_dynamic-slice_fusion
  308.0 0.8 copy.14
Async XLA Ops:
  7.2 1.6 copy-start
  7.2 299.5 %all-reduce.5.cloned.1.call-start = ((), (), s32[]{:S(2)}) async-start(), calls=%async_computation | async-start | bytes 8388608
  8.8 4.3 %copy-start.2 = (bf16[8,1024]{1,0:T(8,128)(2,1)S(1)}, bf16[8,1024]{1,0:T(8,128)(2,1)}, u32[]{:S(2)}) copy-start(bf16[8,1024]{1,0:T(8,128)(2,1)} %param.10) | copy-start | bytes 49156
  8.8 4.3 %copy-start.4 = (f32[8]{0:T(128)S(1)}, f32[8]{0:T(128)}, u32[]{:S(2)}) copy-start(f32[8]{0:T(128)} %param.11) | copy-start | bytes 100
  8.8 18.0 %copy-start.3 = (f32[8,512]{1,0:T(8,128)S(1)}, f32[8,512]{1,0:T(8,128)}, u32[]{:S(2)}) copy-start(f32[8,512]{1,0:T(8,128)} %param.12) | copy-start | bytes 49156
  8.8 18.0 %copy-start.5 = (f32[8]{0:T(128)S(1)}, f32[8]{0:T(128)}, u32[]{:S(2)}) copy-start(f32[8]{0:T(128)} %param.13) | copy-start | bytes 100
  8.8 18.2 %copy-start.6 = (f32[1024]{0:T(1024)S(1)}, f32[1024]{0:T(1024)}, u32[]{:S(2)}) copy-start(f32[1024]{0:T(1024)} %param.9) | copy-start | bytes 12292
  13.0 16.2 %copy-start.1 = (bf16[1024,1024]{1,0:T(8,128)(2,1)}, bf16[1024,1024]{1,0:T(8,128)(2,1)S(1)}, u32[]{:S(2)}) copy-start(bf16[1024,1024]{1,0:T(8,128)(2,1)S(1)} %get-tuple-element.25) | copy-start | bytes 6291460
  29.3 1.4 copy-start.7
Sparse Core Ops, SparseCore 0:
  35.1 271.5 all-reduce.4
where the time goes:
time: 316 us
  waiting for transfers between devices  183 us (58%)
  blocking collectives  92.7 us (29%)
  matrix products  19.4 us (6%)
  between operations  14.1 us (4%)
  local copies, waits for them, and re-layouts  5.57 us (2%)
    unnamed x2, waiting for transfers between devices  183 us
    unnamed x1, blocking collectives  79.8 us
    all_gather x1, blocking collectives, shards(): everyone = lax.all_gather(predicted, 'member', axis=0, tiled=True)  12.9 us
  transfers between devices with their start and end apart: 1, of which 1 were waited for; matrix products, arithmetic and copies ran while one was open for 3% of the time, Pallas kernels for 0%

commit v1 on v0

v1 whole, which is shorter than its diff:
```python
import functools

import jax
import jax.numpy as jnp
from jax import lax
from jax.experimental import pallas as pl
from jax.experimental.pallas import tpu as pltpu
from jax.sharding import PartitionSpec as P

MESH = pl.DeviceIdType.MESH
BF = jnp.bfloat16
F32 = jnp.float32

ALPHA = 0.95
DELTA_SQ = 0.0025
INV_ROOT2 = 0.7071067811865476
INV_ROOT2PI = 0.3989422804014327
HALF_LOG2E = 0.5 * 1.4426950408889634

MEMBERS = 16
EPS_SHARE = (1.0 - ALPHA) / MEMBERS
FACTOR = (1.0 - EPS_SHARE) / (MEMBERS * (MEMBERS - 1))

CHUNKS = (0, 1, 0, 1)
CW = 256


def dg(a, b, ca, cb):
    return lax.dot_general(a, b, (((ca,), (cb,)), ((), ())), preferred_element_type=F32)


def rsum(parts):
    total = parts[0]
    for p in parts[1:]:
        total = total + p
    return total


def kernel(
    x_hbm, w_hbm, bin_ref, wo_ref, bout_ref, tgt_ref, vw_ref,
    gi_ref, gw_ref, gbi_ref, gwo_ref, gbo_ref,
    xv, wv, act, slope, bp, grad, bcol, ev,
    gp, go, r0, r1, s2, r2, zs, zr, pay, ar0, ar1, ar2, ar3, fin, stage,
    ld_sem, ev_ss, ev_rs, c_ss, c_rs, s1_ss, s1_rs, s2_ss, s2_rs, z_ss, z_rs,
    a_ss, a_rs, st_sem,
):
    mem = lax.axis_index("member")
    spc = lax.axis_index("space")
    x, c = mem // 2, mem % 2
    y, z = spc // 8, spc % 8

    def dx(d):
        return (lax.rem(x + d, 4) * 2 + c, spc)

    def dy(d):
        return (mem, lax.rem(y + d, 4) * 8 + z)

    def dz(d):
        return (mem, y * 8 + lax.rem(z + d, 8))

    partner = (x * 2 + 1 - c, spc)

    barrier = pltpu.get_barrier_semaphore()
    for d in range(1, 8):
        pl.semaphore_signal(barrier, inc=1, device_id=(lax.rem(mem + d, 8), spc), device_id_type=MESH)
        pl.semaphore_signal(barrier, inc=1, device_id=dz(d), device_id_type=MESH)
    for d in range(1, 4):
        pl.semaphore_signal(barrier, inc=1, device_id=dy(d), device_id_type=MESH)

    sends = []

    def send(src, dst, ssem, rsem, dev):
        cp = pltpu.make_async_remote_copy(
            src_ref=src, dst_ref=dst, send_sem=ssem, recv_sem=rsem, device_id=dev, device_id_type=MESH
        )
        cp.start()
        sends.append(cp)
        return cp

    loads = []
    cp = pltpu.make_async_copy(w_hbm, wv, ld_sem.at[4])
    cp.start()
    for i, r in enumerate((0, 512, 256, 768)):
        k = pltpu.make_async_copy(x_hbm.at[pl.ds(r, 256), :], xv.at[pl.ds(r, 256), :], ld_sem.at[i])
        k.start()
        loads.append(k)
    cp.wait()

    rows8 = lax.broadcasted_iota(jnp.int32, (8, 128), 0)

    def column(ref):
        out = jnp.zeros((8, 128), F32)
        for v in range(8):
            out = jnp.where(rows8 == v, ref[v], out)
        return jnp.concatenate([out, out], axis=1)

    bout = column(bout_ref)
    vwt = column(vw_ref)

    def forward(r, half, l):
        xr = xv[r : r + 256, :]
        for q in range(0, 1024, 256):
            pre = dg(xr, wv[:, q : q + 256], 1, 0) + bin_ref[:, q : q + 256]
            cdf = 0.5 * (1.0 + lax.erf(pre * INV_ROOT2))
            e = jnp.exp2((pre * pre) * (-HALF_LOG2E))
            act[r : r + 256, q : q + 256] = (pre * cdf).astype(BF)
            slope[r : r + 256, q : q + 256] = cdf + pre * e * INV_ROOT2PI
        ev[half, mem, l] = dg(wo_ref[...], act[r : r + 256, :], 1, 1) + bout

    evs = []
    for half in range(2):
        for l in range(2):
            loads[half * 2 + l].wait()
            forward(l * 512 + half * 256, half, l)
        if half == 0:
            pl.semaphore_wait(barrier, 17)
        cps = []
        for d in range(1, 8):
            cps.append(
                send(ev.at[half, mem], ev.at[half, mem], ev_ss.at[half, d - 1], ev_rs.at[half, d - 1],
                     (lax.rem(mem + d, 8), spc))
            )
        evs.append(cps)

    bcol[...] = jnp.zeros((8, 1024), F32)
    gsum = jnp.zeros((8, 128), F32)
    for half in range(2):
        for cp in evs[half]:
            cp.wait_recv()
        tgt = tgt_ref[:, half * 256 : half * 256 + 256]
        for l in range(2):
            mine = ev[half, mem, l]
            spread = jnp.zeros((8, 256), F32)
            for k in range(16):
                df = mine - ev[half, k // 2, k % 2]
                spread = spread + df * lax.rsqrt(df * df + DELTA_SQ)
            miss = mine - tgt
            direct = miss * lax.rsqrt(miss * miss + DELTA_SQ)
            g = vwt * (direct * (1.0 / MEMBERS) - FACTOR * spread)
            gsum = gsum + g[:, :128] + g[:, 128:]
            r = l * 512 + half * 256
            grad[:, r : r + 256] = g
            gb = g.astype(BF)
            for q in range(0, 1024, 256):
                ba = dg(gb, wo_ref[:, q : q + 256], 0, 0)
                p = (ba * slope[r : r + 256, q : q + 256]).astype(BF)
                bp[r : r + 256, q : q + 256] = p
                bcol[:, q : q + 256] += jnp.sum(p.astype(F32).reshape(32, 8, 256), axis=0)

    def lhs(core):
        return jnp.concatenate(
            [xv[:, pl.ds(pl.multiple_of(xx * 256 + core * 128, 128), 128)] for xx in range(4)], axis=1
        )

    def product(ref, s, core):
        ref[s] = dg(lhs(core), bp[:, s * CW : (s + 1) * CW], 0, 0).reshape(4, 4, 32, CW)

    s1 = [None] * 4
    cc = [None] * 4
    for pair in ((0, 1), (2, 3)):
        for s in pair:
            product(gp, s, 1 - c)
            cc[s] = send(gp.at[s], r0.at[s], c_ss.at[s], c_rs.at[s], partner)
        for s in pair:
            product(go, s, c)
        for s in pair:
            cc[s].wait_recv()
            go[s] = go[s] + r0[s]
            s1[s] = []
            for d in (2, 1, 3):
                if CHUNKS[s] == 0:
                    src, dev = go.at[s, lax.rem(x + d, 4)], dx(d)
                else:
                    src, dev = go.at[s, :, lax.rem(y + d, 4)], dy(d)
                s1[s].append(send(src, r1.at[s, d - 1], s1_ss.at[s, d - 1], s1_rs.at[s, d - 1], dev))

    for q in range(0, 1024, 256):
        t = dg(grad[...].astype(BF), act[:, q : q + 256], 1, 0)
        pay[q // 128] = t[:, :128]
        pay[q // 128 + 1] = t[:, 128:]
    pay[8] = gsum
    colsum = jnp.sum(bcol[...], axis=0, keepdims=True)
    for q in range(8):
        pay[9, q : q + 1, :] = colsum[:, q * 128 : (q + 1) * 128]
    for q in range(10, 16):
        pay[q] = jnp.zeros((8, 128), F32)
    a0 = send(pay.at[pl.ds((1 - c) * 8, 8)], ar0, a_ss.at[0], a_rs.at[0], partner)

    def d_block(b):
        for q in range(0, 1024, 256):
            stage[b * 256 : b * 256 + 256, q : q + 256] = dg(
                bp[b * 256 : b * 256 + 256, :], wv[q : q + 256, :], 1, 1
            ).astype(BF)
        out = pltpu.make_async_copy(
            stage.at[pl.ds(b * 256, 256), :], gi_ref.at[pl.ds(b * 256, 256), :], st_sem.at[b]
        )
        out.start()
        return out

    outs = [d_block(0)]

    a0.wait_recv()
    ar1[...] = pay[pl.ds(c * 8, 8)] + ar0[...]
    a1 = [send(ar1.at[pl.ds(lax.rem(x + d, 4) * 2, 2)], ar2.at[d - 1], a_ss.at[d], a_rs.at[d], dx(d)) for d in (2, 1, 3)]
    outs.append(d_block(1))
    for cp in a1:
        cp.wait_recv()
    mine = ar1[pl.ds(x * 2, 2)] + rsum([ar2[i] for i in range(3)])
    ar3[0] = mine
    a2 = [send(ar3.at[0], ar3.at[d], a_ss.at[3 + d], a_rs.at[3 + d], dy(d)) for d in (2, 1, 3)]
    outs.append(d_block(2))
    for cp in a2:
        cp.wait_recv()
    ar3[4] = rsum([ar3[i] for i in range(4)])
    a3 = [send(ar3.at[4], ar3.at[4 + d], a_ss.at[6 + d], a_rs.at[6 + d], dz(d)) for d in (4, 3, 5, 2, 6, 1, 7)]
    outs.append(d_block(3))

    def stage2(s):
        for cp in s1[s]:
            cp.wait_recv()
        if CHUNKS[s] == 0:
            s2[s] = go[s, x] + rsum([r1[s, i] for i in range(3)])
        else:
            s2[s] = go[s, :, y] + rsum([r1[s, i] for i in range(3)])
        out = []
        for d in (2, 1, 3):
            if CHUNKS[s] == 0:
                src, dev = s2.at[s, lax.rem(y + d, 4)], dy(d)
            else:
                src, dev = s2.at[s, lax.rem(x + d, 4)], dx(d)
            out.append(send(src, r2.at[s, d - 1], s2_ss.at[s, d - 1], s2_rs.at[s, d - 1], dev))
        return out

    low = rows8 < 4

    def stage3(pair, e, waits):
        for j, s in enumerate(pair):
            for cp in waits[j]:
                cp.wait_recv()
            own = y if CHUNKS[s] == 0 else x
            t = s2[s, own] + rsum([r2[s, i] for i in range(3)])
            for p in range(4):
                u = t[8 * p : 8 * p + 8, :128]
                v = t[8 * p : 8 * p + 8, 128:]
                zs[e, 2 * p, j] = jnp.where(low, u, pltpu.roll(v, 4, 0))
                zs[e, 2 * p + 1, j] = jnp.where(low, pltpu.roll(u, 4, 0), v)
        return [
            send(zs.at[e, lax.rem(z + d, 8)], zr.at[e, d - 1], z_ss.at[e, d - 1], z_rs.at[e, d - 1], dz(d))
            for d in (4, 3, 5, 2, 6, 1, 7)
        ]

    def finish(pair, e, waits):
        for cp in waits:
            cp.wait_recv()
        for j, s in enumerate(pair):
            t = zs[e, z, j] + rsum([zr[e, i, j] for i in range(7)])
            gw_ref[:, s * CW : s * CW + 128] = t[0:4]
            gw_ref[:, s * CW + 128 : s * CW + 256] = t[4:8]

    w2a = [stage2(0), stage2(1)]
    for cp in a3:
        cp.wait_recv()
    quarter = pl.ds(c * 8 + x * 2, 2)
    fin[quarter] = rsum([ar3[i] for i in range(4, 12)])
    a4 = [send(fin.at[quarter], fin.at[quarter], a_ss.at[13 + d], a_rs.at[13 + d], dx(d)) for d in (2, 1, 3)]
    w3a = stage3((0, 1), 0, w2a)
    w2b = [stage2(2), stage2(3)]
    for cp in a4:
        cp.wait_recv()
    half_fin = fin.at[pl.ds(c * 8, 8)]
    a5 = send(half_fin, half_fin, a_ss.at[17], a_rs.at[17], partner)
    finish((0, 1), 0, w3a)
    w3b = stage3((2, 3), 1, w2b)
    a5.wait_recv()
    for q in range(8):
        gwo_ref[:, q * 128 : (q + 1) * 128] = fin[q]
    bo = jnp.sum(fin[8], axis=1, keepdims=True)
    for v in range(8):
        gbo_ref[v] = jnp.sum(jnp.where(rows8[:, :1] == v, bo, 0.0))
    lanes = lax.broadcasted_iota(jnp.int32, (8, 128), 1)
    bi = fin[9]
    for r in range(4):
        gbi_ref[r] = jnp.sum(jnp.where((rows8 == mem) & (lanes == spc * 4 + r), bi, 0.0))
    finish((2, 3), 1, w3b)
    for cp in sends:
        cp.wait_send()
    for cp in outs:
        cp.wait()


def shards(inputs, weight_in, bias_in, weight_out, bias_out, target_field, variable_weight):
    rows = inputs.reshape(1024, 1024)
    vm = pl.BlockSpec(memory_space=pltpu.VMEM)
    sm = pl.BlockSpec(memory_space=pltpu.SMEM)
    hb = pl.BlockSpec(memory_space=pl.ANY)
    dma = pltpu.SemaphoreType.DMA
    gi, gw, gbi, gwo, gbo = pl.pallas_call(
        kernel,
        out_shape=(
            jax.ShapeDtypeStruct((1024, 1024), BF),
            jax.ShapeDtypeStruct((4, 1024), F32),
            jax.ShapeDtypeStruct((4,), F32),
            jax.ShapeDtypeStruct((8, 1024), F32),
            jax.ShapeDtypeStruct((8,), F32),
        ),
        in_specs=[hb, hb, vm, vm, sm, vm, sm],
        out_specs=(hb, vm, sm, vm, sm),
        scratch_shapes=[
            pltpu.VMEM((1024, 1024), BF),
            pltpu.VMEM((1024, 1024), BF),
            pltpu.VMEM((1024, 1024), BF),
            pltpu.VMEM((1024, 1024), F32),
            pltpu.VMEM((1024, 1024), BF),
            pltpu.VMEM((8, 1024), F32),
            pltpu.VMEM((8, 1024), F32),
            pltpu.VMEM((2, 8, 2, 8, 256), F32),
            pltpu.VMEM((4, 4, 4, 32, CW), F32),
            pltpu.VMEM((4, 4, 4, 32, CW), F32),
            pltpu.VMEM((4, 4, 4, 32, CW), F32),
            pltpu.VMEM((4, 3, 4, 32, CW), F32),
            pltpu.VMEM((4, 4, 32, CW), F32),
            pltpu.VMEM((4, 3, 32, CW), F32),
            pltpu.VMEM((2, 8, 2, 8, 128), F32),
            pltpu.VMEM((2, 7, 2, 8, 128), F32),
            pltpu.VMEM((16, 8, 128), F32),
            pltpu.VMEM((8, 8, 128), F32),
            pltpu.VMEM((8, 8, 128), F32),
            pltpu.VMEM((3, 2, 8, 128), F32),
            pltpu.VMEM((12, 2, 8, 128), F32),
            pltpu.VMEM((16, 8, 128), F32),
            pltpu.VMEM((1024, 1024), BF),
            dma((5,)),
            dma((2, 7)), dma((2, 7)),
            dma((4,)), dma((4,)),
            dma((4, 3)), dma((4, 3)),
            dma((4, 3)), dma((4, 3)),
            dma((2, 7)), dma((2, 7)),
            dma((18,)), dma((18,)),
            dma((4,)),
        ],
        compiler_params=pltpu.CompilerParams(
            collective_id=0, has_side_effects=True, vmem_limit_bytes=48 * 2**20
        ),
        cost_estimate=pl.CostEstimate(flops=6 * 2**30, bytes_accessed=7 * 2**20, transcendentals=2 * 2**20),
        name="crps_backward",
    )(rows, weight_in, bias_in.reshape(1, 1024), weight_out, bias_out, target_field, variable_weight)
    return gi.reshape(2, 512, 1024), gw, gbi, gwo, gbo


def solution(mesh):
    placed = (P("member", "space", None), P(), P(), P(), P(), P(None, "space"), P())
    return jax.shard_map(
        shards,
        mesh=mesh,
        in_specs=placed,
        out_specs=(
            P("member", "space", None),
            P(("member", "space"), None),
            P(("member", "space")),
            P(),
            P(),
        ),
        check_vma=False,
    )
```

time: 316 us -> 62.8 us (0.20)
  waiting for transfers between devices: 183 us -> 0 us
  blocking collectives: 92.7 us -> 0 us
  Pallas kernels: 0 us -> 53.3 us
  matrix products: 19.4 us -> 0 us
  between operations: 14.1 us -> 0.66 us
    unnamed x2 -> x0, waiting for transfers between devices: 183 us -> none
    unnamed x1 -> x0, blocking collectives: 79.8 us -> none
    pallas_call x0 -> x1, Pallas kernels: none -> 53.3 us  [shards(): pl.pallas_call(kernel, out_shape=(jax.ShapeDtypeStruct((1024, 1024), BF),...]
    dot_general x6 -> x0, matrix products: 19.4 us -> none  [the longest x1 5.92 us: shards(): lax.dot_general(back_pre, weight_in, (((1,), (1,)), ((), ())), preferred_...]
    all_gather x1 -> x0, blocking collectives: 12.9 us -> none  [shards(): everyone = lax.all_gather(predicted, 'member', axis=0, tiled=True)]
    unnamed x19 -> x17, local copies, waits for them, and re-layouts: 5.57 us -> 8.58 us
  transfers between devices with their start and end apart: 1 -> 0, of which waited for: 1 -> 0; matrix products, arithmetic and copies ran while one was open for 3% -> 0% of each run, Pallas kernels for 0% -> 0%
where the time goes in v1:
time: 62.8 us; the launch traced here: 62.5 us
  Pallas kernels  53.3 us (85%)
  local copies, waits for them, and re-layouts  8.58 us (14%)
  between operations  0.66 us (1%)
    pallas_call x1, Pallas kernels, shards(): pl.pallas_call(kernel, out_shape=(jax.ShapeDtypeStruct((1024, 1024), BF),...  53.3 us
    unnamed x17, local copies, waits for them, and re-layouts  8.58 us

profile of v1, /device:TPU:2, one launch (start us, length us, event | category | flops | bytes accessed | tf_op | source)
XLA Modules:
  0.0 62.5 jit_solution(7985203624042764448)
XLA Ops:
  0.6 0.0 copy-start
  0.6 1.6 %copy-done = bf16[2,512,1024]{2,1,0:T(8,128)(2,1)S(1)} copy-done((bf16[2,512,1024]{2,1,0:T(8,128)(2,1)S(1)}, bf16[2,512,1024]{2,1,0:T(8,128)(2,1)}, u32[]{:S(2)}) %copy-start) | copy-done | bytes 2097176
  2.2 0.0 copy-start.1
  2.2 0.7 %copy-done.1 = bf16[8,1024]{1,0:T(8,128)(2,1)S(1)} copy-done((bf16[8,1024]{1,0:T(8,128)(2,1)S(1)}, bf16[8,1024]{1,0:T(8,128)(2,1)}, u32[]{:S(2)}) %copy-start.1) | copy-done | bytes 16408
  2.9 0.0 copy-start.2
  2.9 0.7 %copy-done.2 = f32[8,512]{1,0:T(8,128)S(1)} copy-done((f32[8,512]{1,0:T(8,128)S(1)}, f32[8,512]{1,0:T(8,128)}, u32[]{:S(2)}) %copy-start.2) | copy-done | bytes 16408
  3.7 0.0 copy-start.3
  3.7 0.7 %copy-done.3 = f32[1024]{0:T(1024)S(1)} copy-done((f32[1024]{0:T(1024)S(1)}, f32[1024]{0:T(1024)}, u32[]{:S(2)}) %copy-start.3) | copy-done | bytes 4120
  4.3 0.0 copy-start.4
  4.4 0.7 %copy-done.4 = f32[8]{0:T(128)S(1)} copy-done((f32[8]{0:T(128)S(1)}, f32[8]{0:T(128)}, u32[]{:S(2)}) %copy-start.4) | copy-done | bytes 56
  5.0 0.0 copy-start.5
  5.0 0.7 %copy-done.5 = f32[8]{0:T(128)S(1)} copy-done((f32[8]{0:T(128)S(1)}, f32[8]{0:T(128)}, u32[]{:S(2)}) %copy-start.5) | copy-done | bytes 56
  5.7 53.3 %crps_backward.1 = (bf16[1024,1024]{1,0:T(8,128)(2,1)S(1)}, f32[4,1024]{1,0:T(4,128)S(1)}, f32[4]{0:T(128)S(1)}, f32[8,1024]{1,0:T(8,128)S(1)}, f32[8]{0:T(128)S(1)}) custom-call(bf16[1024,1024]{1,0:T(8,128)(2,1)S(1)} %bitcast.4, bf16[1024,1024]{1,0:T(8,128)(2,1)} %w_hbm.1, f32[1,1024]{1,0:T(1,128)S(1)} %bitcast.5, bf16[8,1024]{1,0:T(8,128)(2,1)S(1)} %copy-done.1, ...), custom_call_target="tpu_custom_call" | custom-call | flops 6442450944 | bytes 7340032 | tf_op jit(solution)/shard_map/crps_backward/pallas_call | solution.py:297
  58.9 1.3 %copy.17 = bf16[2,512,1024]{2,1,0:T(8,128)(2,1)} copy(bf16[2,512,1024]{2,1,0:T(8,128)(2,1)S(1)} %bitcast.3) | data formatting | bytes 4194304
  60.2 0.6 copy.18
  60.8 0.5 copy.19
  61.4 0.6 copy.20
  62.0 0.5 copy.21
Async XLA Ops:
  0.6 1.6 %copy-start = (bf16[2,512,1024]{2,1,0:T(8,128)(2,1)S(1)}, bf16[2,512,1024]{2,1,0:T(8,128)(2,1)}, u32[]{:S(2)}) copy-start(bf16[2,512,1024]{2,1,0:T(8,128)(2,1)} %param.7) | copy-start | bytes 6291460
  2.2 0.7 %copy-start.1 = (bf16[8,1024]{1,0:T(8,128)(2,1)S(1)}, bf16[8,1024]{1,0:T(8,128)(2,1)}, u32[]{:S(2)}) copy-start(bf16[8,1024]{1,0:T(8,128)(2,1)} %wo_ref.1) | copy-start | bytes 49156
  2.9 0.7 %copy-start.2 = (f32[8,512]{1,0:T(8,128)S(1)}, f32[8,512]{1,0:T(8,128)}, u32[]{:S(2)}) copy-start(f32[8,512]{1,0:T(8,128)} %tgt_ref.1) | copy-start | bytes 49156
  3.7 0.7 %copy-start.3 = (f32[1024]{0:T(1024)S(1)}, f32[1024]{0:T(1024)}, u32[]{:S(2)}) copy-start(f32[1024]{0:T(1024)} %param.9) | copy-start | bytes 12292
  4.3 0.7 %copy-start.4 = (f32[8]{0:T(128)S(1)}, f32[8]{0:T(128)}, u32[]{:S(2)}) copy-start(f32[8]{0:T(128)} %bout_ref.1) | copy-start | bytes 100
  5.0 0.7 %copy-start.5 = (f32[8]{0:T(128)S(1)}, f32[8]{0:T(128)}, u32[]{:S(2)}) copy-start(f32[8]{0:T(128)} %vw_ref.1) | copy-start | bytes 100

commit v2 on v1

v2 whole, which is shorter than its diff:
```python
import functools

import jax
import jax.numpy as jnp
from jax import lax
from jax.experimental import pallas as pl
from jax.experimental.pallas import tpu as pltpu
from jax.sharding import PartitionSpec as P

MESH = pl.DeviceIdType.MESH
BF = jnp.bfloat16
F32 = jnp.float32

ALPHA = 0.95
DELTA_SQ = 0.0025
INV_ROOT2 = 0.7071067811865476
INV_ROOT2PI = 0.3989422804014327
HALF_LOG2E = 0.5 * 1.4426950408889634

MEMBERS = 16
EPS_SHARE = (1.0 - ALPHA) / MEMBERS
FACTOR = (1.0 - EPS_SHARE) / (MEMBERS * (MEMBERS - 1))

CHUNKS = (0, 1, 0, 1)
CW = 256


def dg(a, b, ca, cb):
    return lax.dot_general(a, b, (((ca,), (cb,)), ((), ())), preferred_element_type=F32)


def rsum(parts):
    total = parts[0]
    for p in parts[1:]:
        total = total + p
    return total


def kernel(
    x_hbm, w_hbm, bin_hbm, wo_hbm, bout_hbm, tgt_hbm, vw_hbm,
    gi_ref, gw_ref, gbi_ref, gwo_ref, gbo_ref,
    bin_ref, wo_ref, bout_ref, tgt_ref, vw_ref, xv, wv, act, slope, bp, grad, bcol, ev,
    gp, go, r0, r1, s2, r2, zs, zr, pay, ar0, ar1, ar2, ar3, fin, stage,
    ld_sem, ev_ss, ev_rs, c_ss, c_rs, s1_ss, s1_rs, s2_ss, s2_rs, z_ss, z_rs,
    a_ss, a_rs, st_sem,
):
    mem = lax.axis_index("member")
    spc = lax.axis_index("space")
    x, c = mem // 2, mem % 2
    y, z = spc // 8, spc % 8

    def dx(d):
        return (lax.rem(x + d, 4) * 2 + c, spc)

    def dy(d):
        return (mem, lax.rem(y + d, 4) * 8 + z)

    def dz(d):
        return (mem, y * 8 + lax.rem(z + d, 8))

    partner = (x * 2 + 1 - c, spc)

    sends = []

    def remote(src, dst, ssem, rsem, dev):
        return pltpu.make_async_remote_copy(
            src_ref=src, dst_ref=dst, send_sem=ssem, recv_sem=rsem, device_id=dev, device_id_type=MESH
        )

    def send(src, dst, ssem, rsem, dev):
        cp = remote(src, dst, ssem, rsem, dev)
        cp.start()
        sends.append(cp)
        return cp

    xloads, wloads = [], []
    for i, r in enumerate((0, 512, 256, 768)):
        xloads.append(
            pltpu.make_async_copy(x_hbm.at[pl.ds(r, 256), :], xv.at[pl.ds(i * 256, 256), :], ld_sem.at[i])
        )
    for i in range(4):
        part = pl.ds(i * 256, 256)
        wloads.append(pltpu.make_async_copy(w_hbm.at[part, :], wv.at[part, :], ld_sem.at[4 + i]))
    for k in [xloads[0]] + wloads + xloads[1:]:
        k.start()
    small = [
        pltpu.make_async_copy(src, dst, ld_sem.at[8 + i])
        for i, (src, dst) in enumerate(
            ((bin_hbm, bin_ref), (wo_hbm, wo_ref), (bout_hbm, bout_ref), (tgt_hbm, tgt_ref), (vw_hbm, vw_ref))
        )
    ]
    for k in small:
        k.start()

    barrier = pltpu.get_barrier_semaphore()
    for d in range(1, 8):
        pl.semaphore_signal(barrier, inc=1, device_id=(lax.rem(mem + d, 8), spc), device_id_type=MESH)
        pl.semaphore_signal(barrier, inc=1, device_id=dz(d), device_id_type=MESH)
    for d in range(1, 4):
        pl.semaphore_signal(barrier, inc=1, device_id=dy(d), device_id_type=MESH)

    for k in small:
        k.wait()

    rows8 = lax.broadcasted_iota(jnp.int32, (8, 128), 0)

    def column(ref):
        out = jnp.zeros((8, 128), F32)
        for v in range(8):
            out = jnp.where(rows8 == v, ref[v], out)
        return jnp.concatenate([out, out], axis=1)

    bout = column(bout_ref)
    vwt = column(vw_ref)

    for k in wloads:
        k.wait()

    def gather(half, d):
        blk = ev.at[half, mem]
        return remote(blk, blk, ev_ss.at[half, d - 1], ev_rs.at[half, d - 1], (lax.rem(mem + d, 8), spc))

    def forward(i, carry):
        r = pl.ds(pl.multiple_of(i * 256, 256), 256)
        pltpu.make_async_copy(x_hbm.at[pl.ds(0, 256), :], xv.at[r, :], ld_sem.at[i]).wait()
        xr = xv[r, :]
        for q in range(0, 1024, 256):
            pre = dg(xr, wv[:, q : q + 256], 1, 0) + bin_ref[:, q : q + 256]
            cdf = 0.5 * (1.0 + lax.erf(pre * INV_ROOT2))
            e = jnp.exp2((pre * pre) * (-HALF_LOG2E))
            act[r, q : q + 256] = (pre * cdf).astype(BF)
            slope[r, q : q + 256] = cdf + pre * e * INV_ROOT2PI
        ev[i // 2, mem, lax.rem(i, 2)] = dg(wo_ref[...], act[r, :], 1, 1) + bout
        return carry

    for half in range(2):
        lax.fori_loop(2 * half, 2 * half + 2, forward, 0)
        if half == 0:
            pl.semaphore_wait(barrier, 17)
        for d in range(1, 8):
            cp = gather(half, d)
            cp.start()
            sends.append(cp)

    bcol[...] = jnp.zeros((8, 1024), F32)
    gsum = jnp.zeros((8, 128), F32)

    def backward(i, gsum):
        half, l = i // 2, lax.rem(i, 2)
        tgt = tgt_ref[:, pl.ds(pl.multiple_of(half * 256, 256), 256)]
        mine = ev[half, mem, l]
        spread = jnp.zeros((8, 256), F32)
        for k in range(16):
            df = mine - ev[half, k // 2, k % 2]
            spread = spread + df * lax.rsqrt(df * df + DELTA_SQ)
        miss = mine - tgt
        direct = miss * lax.rsqrt(miss * miss + DELTA_SQ)
        g = vwt * (direct * (1.0 / MEMBERS) - FACTOR * spread)
        r = pl.ds(pl.multiple_of(i * 256, 256), 256)
        grad[:, r] = g
        gb = g.astype(BF)
        for q in range(0, 1024, 256):
            ba = dg(gb, wo_ref[:, q : q + 256], 0, 0)
            p = (ba * slope[r, q : q + 256]).astype(BF)
            bp[r, q : q + 256] = p
            bcol[:, q : q + 256] += jnp.sum(p.astype(F32).reshape(32, 8, 256), axis=0)
        return gsum + g[:, :128] + g[:, 128:]

    def product(s, core, half):
        r = pl.ds(half * 512, 512)
        lhs = jnp.concatenate(
            [xv[r, pl.ds(pl.multiple_of(xx * 256 + core * 128, 128), 128)] for xx in range(4)], axis=1
        )
        return dg(lhs, bp[r, pl.ds(pl.multiple_of(s * CW, CW), CW)], 0, 0).reshape(4, 4, 32, CW)

    for d in range(1, 8):
        gather(0, d).wait_recv()
    gsum = lax.fori_loop(0, 2, backward, gsum)

    def early(s, carry):
        gp[s] = product(s, 1 - c, 0)
        go[s] = product(s, c, 0)
        return carry

    lax.fori_loop(0, 4, early, 0)
    for d in range(1, 8):
        gather(1, d).wait_recv()
    gsum = lax.fori_loop(2, 4, backward, gsum)

    def cross(s):
        return remote(gp.at[s], r0.at[s], c_ss.at[s], c_rs.at[s], partner)

    def first(s, axis, d):
        if axis == 0:
            src, dev = go.at[s, lax.rem(x + d, 4)], dx(d)
        else:
            src, dev = go.at[s, :, lax.rem(y + d, 4)], dy(d)
        return remote(src, r1.at[s, d - 1], s1_ss.at[s, d - 1], s1_rs.at[s, d - 1], dev)

    def late(s, carry):
        gp[s] += product(s, 1 - c, 1)
        cross(s).start()
        return carry

    lax.fori_loop(0, 4, late, 0)

    for q in range(0, 1024, 256):
        t = dg(grad[...].astype(BF), act[:, q : q + 256], 1, 0)
        pay[q // 128] = t[:, :128]
        pay[q // 128 + 1] = t[:, 128:]
    pay[8] = gsum
    colsum = jnp.sum(bcol[...], axis=0, keepdims=True)
    for q in range(8):
        pay[9, q : q + 1, :] = colsum[:, q * 128 : (q + 1) * 128]
    for q in range(10, 16):
        pay[q] = jnp.zeros((8, 128), F32)
    a0 = send(pay.at[pl.ds((1 - c) * 8, 8)], ar0, a_ss.at[0], a_rs.at[0], partner)

    def later(p, carry):
        for axis in range(2):
            s = 2 * p + axis
            go[s] += product(s, c, 1)
            cross(s).wait_recv()
            go[s] += r0[s]
            for d in (2, 1, 3):
                first(s, axis, d).start()
        return carry

    lax.fori_loop(0, 2, later, 0)
    sends += [cross(s) for s in range(4)]
    s1 = [[first(s, CHUNKS[s], d) for d in (2, 1, 3)] for s in range(4)]
    for group in s1:
        sends += group

    def out_copy(b):
        r = lax.rem(b, 2) * 512 + (b // 2) * 256
        return pltpu.make_async_copy(
            stage.at[pl.ds(pl.multiple_of(b * 256, 256), 256), :],
            gi_ref.at[pl.ds(pl.multiple_of(r, 256), 256), :],
            st_sem.at[b],
        )

    def d_block(b, carry):
        r = pl.ds(pl.multiple_of(b * 256, 256), 256)
        for q in range(0, 1024, 256):
            stage[r, q : q + 256] = dg(bp[r, :], wv[q : q + 256, :], 1, 1).astype(BF)
        out_copy(b).start()
        return carry

    a0.wait_recv()
    ar1[...] = pay[pl.ds(c * 8, 8)] + ar0[...]
    a1 = [
        send(ar1.at[lax.rem(z + d, 8)], ar2.at[d - 1], a_ss.at[d], a_rs.at[d], dz(d)) for d in (4, 3, 5, 2, 6, 1, 7)
    ]
    lax.fori_loop(0, 4, d_block, 0)
    for cp in a1:
        cp.wait_recv()
    ar3[0] = ar1[z] + rsum([ar2[i] for i in range(7)])
    a2 = [send(ar3.at[0], ar3.at[d], a_ss.at[7 + d], a_rs.at[7 + d], dx(d)) for d in (2, 1, 3)]

    def stage2(s):
        for cp in s1[s]:
            cp.wait_recv()
        if CHUNKS[s] == 0:
            s2[s] = go[s, x] + rsum([r1[s, i] for i in range(3)])
        else:
            s2[s] = go[s, :, y] + rsum([r1[s, i] for i in range(3)])
        out = []
        for d in (2, 1, 3):
            if CHUNKS[s] == 0:
                src, dev = s2.at[s, lax.rem(y + d, 4)], dy(d)
            else:
                src, dev = s2.at[s, lax.rem(x + d, 4)], dx(d)
            out.append(send(src, r2.at[s, d - 1], s2_ss.at[s, d - 1], s2_rs.at[s, d - 1], dev))
        return out

    low = rows8 < 4

    def stage3(pair, e, waits):
        for j, s in enumerate(pair):
            for cp in waits[j]:
                cp.wait_recv()
            own = y if CHUNKS[s] == 0 else x
            t = s2[s, own] + rsum([r2[s, i] for i in range(3)])
            for p in range(4):
                u = t[8 * p : 8 * p + 8, :128]
                v = t[8 * p : 8 * p + 8, 128:]
                zs[e, 2 * p, j] = jnp.where(low, u, pltpu.roll(v, 4, 0))
                zs[e, 2 * p + 1, j] = jnp.where(low, pltpu.roll(u, 4, 0), v)
        return [
            send(zs.at[e, lax.rem(z + d, 8)], zr.at[e, d - 1], z_ss.at[e, d - 1], z_rs.at[e, d - 1], dz(d))
            for d in (4, 3, 5, 2, 6, 1, 7)
        ]

    def finish(pair, e, waits):
        for cp in waits:
            cp.wait_recv()
        for j, s in enumerate(pair):
            t = zs[e, z, j] + rsum([zr[e, i, j] for i in range(7)])
            gw_ref[:, s * CW : s * CW + 128] = t[0:4]
            gw_ref[:, s * CW + 128 : s * CW + 256] = t[4:8]

    w2 = [stage2(s) for s in range(4)]
    for cp in a2:
        cp.wait_recv()
    ar3[4] = rsum([ar3[i] for i in range(4)])
    a3 = [send(ar3.at[4], ar3.at[4 + d], a_ss.at[10 + d], a_rs.at[10 + d], dy(d)) for d in (2, 1, 3)]
    w3a = stage3((0, 1), 0, w2[:2])
    for cp in a3:
        cp.wait_recv()
    own = fin.at[c * 8 + z]
    fin[c * 8 + z] = rsum([ar3[i] for i in range(4, 8)])
    a4 = [send(own, own, a_ss.at[13 + d], a_rs.at[13 + d], dz(d)) for d in (4, 3, 5, 2, 6, 1, 7)]
    w3b = stage3((2, 3), 1, w2[2:])
    finish((0, 1), 0, w3a)
    for cp in a4:
        cp.wait_recv()
    half_fin = fin.at[pl.ds(c * 8, 8)]
    a5 = send(half_fin, half_fin, a_ss.at[21], a_rs.at[21], partner)
    a5.wait_recv()
    for q in range(8):
        gwo_ref[:, q * 128 : (q + 1) * 128] = fin[q]
    bo = jnp.sum(fin[8], axis=1, keepdims=True)
    for v in range(8):
        gbo_ref[v] = jnp.sum(jnp.where(rows8[:, :1] == v, bo, 0.0))
    lanes = lax.broadcasted_iota(jnp.int32, (8, 128), 1)
    bi = fin[9]
    for r in range(4):
        gbi_ref[r] = jnp.sum(jnp.where((rows8 == mem) & (lanes == spc * 4 + r), bi, 0.0))
    finish((2, 3), 1, w3b)
    for cp in sends:
        cp.wait_send()
    for b in range(4):
        out_copy(b).wait()


def place(*refs):
    src, dst, mid, sem, sem2 = refs[:5], refs[5:10], refs[10:15], refs[15], refs[16]
    pieces = [(src[0].at[pl.ds(r, 128), :], mid[0].at[pl.ds(r, 128), :], dst[0].at[pl.ds(r, 128), :]) for r in range(0, 1024, 128)]
    pieces += list(zip(src[1:], mid[1:], dst[1:]))
    ins = [pltpu.make_async_copy(a, b, sem.at[i]) for i, (a, b, _) in enumerate(pieces)]
    outs = [pltpu.make_async_copy(b, d, sem2.at[i]) for i, (_, b, d) in enumerate(pieces)]
    for cp in ins:
        cp.start()
    for a, b in zip(ins, outs):
        a.wait()
        b.start()
    for cp in outs:
        cp.wait()


def shards(inputs, weight_in, bias_in, weight_out, bias_out, target_field, variable_weight):
    rows = inputs.reshape(1024, 1024)
    vm = pl.BlockSpec(memory_space=pltpu.VMEM)
    sm = pl.BlockSpec(memory_space=pltpu.SMEM)
    hb = pl.BlockSpec(memory_space=pl.ANY)
    dma = pltpu.SemaphoreType.DMA
    gi, gw, gbi, gwo, gbo = pl.pallas_call(
        kernel,
        out_shape=(
            jax.ShapeDtypeStruct((1024, 1024), BF),
            jax.ShapeDtypeStruct((4, 1024), F32),
            jax.ShapeDtypeStruct((4,), F32),
            jax.ShapeDtypeStruct((8, 1024), F32),
            jax.ShapeDtypeStruct((8,), F32),
        ),
        in_specs=[hb, hb, hb, hb, hb, hb, hb],
        out_specs=(hb, vm, sm, vm, sm),
        scratch_shapes=[
            pltpu.VMEM((1, 1024), F32),
            pltpu.VMEM((8, 1024), BF),
            pltpu.SMEM((8,), F32),
            pltpu.VMEM((8, 512), F32),
            pltpu.SMEM((8,), F32),
            pltpu.VMEM((1024, 1024), BF),
            pltpu.VMEM((1024, 1024), BF),
            pltpu.VMEM((1024, 1024), BF),
            pltpu.VMEM((1024, 1024), F32),
            pltpu.VMEM((1024, 1024), BF),
            pltpu.VMEM((8, 1024), F32),
            pltpu.VMEM((8, 1024), F32),
            pltpu.VMEM((2, 8, 2, 8, 256), F32),
            pltpu.VMEM((4, 4, 4, 32, CW), F32),
            pltpu.VMEM((4, 4, 4, 32, CW), F32),
            pltpu.VMEM((4, 4, 4, 32, CW), F32),
            pltpu.VMEM((4, 3, 4, 32, CW), F32),
            pltpu.VMEM((4, 4, 32, CW), F32),
            pltpu.VMEM((4, 3, 32, CW), F32),
            pltpu.VMEM((2, 8, 2, 8, 128), F32),
            pltpu.VMEM((2, 7, 2, 8, 128), F32),
            pltpu.VMEM((16, 8, 128), F32),
            pltpu.VMEM((8, 8, 128), F32),
            pltpu.VMEM((8, 8, 128), F32),
            pltpu.VMEM((7, 8, 128), F32),
            pltpu.VMEM((8, 8, 128), F32),
            pltpu.VMEM((16, 8, 128), F32),
            pltpu.VMEM((1024, 1024), BF),
            dma((13,)),
            dma((2, 7)), dma((2, 7)),
            dma((4,)), dma((4,)),
            dma((4, 3)), dma((4, 3)),
            dma((4, 3)), dma((4, 3)),
            dma((2, 7)), dma((2, 7)),
            dma((22,)), dma((22,)),
            dma((4,)),
        ],
        compiler_params=pltpu.CompilerParams(
            collective_id=0, has_side_effects=True, vmem_limit_bytes=60 * 2**20
        ),
        cost_estimate=pl.CostEstimate(flops=6 * 2**30, bytes_accessed=7 * 2**20, transcendentals=2 * 2**20),
        name="crps_backward",
    )(rows, weight_in, bias_in.reshape(1, 1024), weight_out, bias_out, target_field, variable_weight)
    outs = pl.pallas_call(
        place,
        out_shape=tuple(jax.ShapeDtypeStruct(a.shape, a.dtype) for a in (gi, gw, gbi, gwo, gbo)),
        in_specs=[hb] * 5,
        out_specs=(hb,) * 5,
        scratch_shapes=[pltpu.VMEM(a.shape, a.dtype) for a in (gi, gw, gbi, gwo, gbo)] + [dma((12,)), dma((12,))],
        compiler_params=pltpu.CompilerParams(vmem_limit_bytes=60 * 2**20),
        name="place",
    )(gi, gw, gbi, gwo, gbo)
    return (outs[0].reshape(2, 512, 1024),) + tuple(outs[1:])


def solution(mesh):
    placed = (P("member", "space", None), P(), P(), P(), P(), P(None, "space"), P())
    return jax.shard_map(
        shards,
        mesh=mesh,
        in_specs=placed,
        out_specs=(
            P("member", "space", None),
            P(("member", "space"), None),
            P(("member", "space")),
            P(),
            P(),
        ),
        check_vma=False,
    )
```

time: 62.8 us -> 51.8 us (0.82)
  the two profiles are of different devices: /device:TPU:2 before, /device:TPU:1 now
where the time goes in v2:
time: 51.8 us; the launch traced here: 51.6 us
  Pallas kernels  51 us (98%)
  between operations  0.64 us (1%)
    pallas_call x1, Pallas kernels, shards(): pl.pallas_call(kernel, out_shape=(jax.ShapeDtypeStruct((1024, 1024), BF),...  48.5 us
    pallas_call x1, Pallas kernels, shards(): pl.pallas_call(place, out_shape=tuple((jax.ShapeDtypeStruct(a.shape, a.dt...  2.48 us

profile of v2, /device:TPU:1, one launch (start us, length us, event | category | flops | bytes accessed | tf_op | source)
XLA Modules:
  0.0 51.6 jit_solution(1970564031854653334)
XLA Ops:
  0.6 48.5 %crps_backward.1 = (bf16[1024,1024]{1,0:T(8,128)(2,1)}, f32[4,1024]{1,0:T(4,128)}, f32[4]{0:T(128)}, f32[8,1024]{1,0:T(8,128)}, f32[8]{0:T(128)}) custom-call(bf16[1024,1024]{1,0:T(8,128)(2,1)} %bitcast.3, bf16[1024,1024]{1,0:T(8,128)(2,1)} %w_hbm.1, f32[1,1024]{1,0:T(1,128)} %bitcast.5, bf16[8,1024]{1,0:T(8,128)(2,1)} %wo_hbm.1, f32[8]{0:T(128)} %bout_hbm.1, ...), custom_call_target="tpu_custom_call" | custom-call | flops 6442450944 | bytes 7340032 | tf_op jit(solution)/shard_map/crps_backward/pallas_call | solution.py:358
  49.2 2.5 %place.1 = (bf16[1024,1024]{1,0:T(8,128)(2,1)}, f32[4,1024]{1,0:T(4,128)}, f32[4]{0:T(128)}, f32[8,1024]{1,0:T(8,128)}, f32[8]{0:T(128)}) custom-call(bf16[1024,1024]{1,0:T(8,128)(2,1)} %get-tuple-element.15.refs_0_, f32[4,1024]{1,0:T(4,128)} %get-tuple-element.16.refs_1_, f32[4]{0:T(128)} %get-tuple-element.17.refs_2_, ...), custom_call_target="tpu_custom_call" | custom-call | tf_op jit(solution)/shard_map/place/pallas_call | solution.py:413

commit v3 on v2

--- a/solution.py
+++ b/solution.py
@@ -21,8 +21,10 @@
 EPS_SHARE = (1.0 - ALPHA) / MEMBERS
 FACTOR = (1.0 - EPS_SHARE) / (MEMBERS * (MEMBERS - 1))
 
-CHUNKS = (0, 1, 0, 1)
 CW = 256
+CHUNKS = ((0, 0, 128, 0), (0, 128, 128, 1), (1, 0, 256, 0), (2, 0, 256, 1), (3, 0, 128, 0), (3, 128, 128, 1))
+NCH = len(CHUNKS)
+ZGROUPS = ((((0, 0), (1, 0)), ((2, 0), (2, 128)), ((3, 0), (3, 128))), (((4, 0), (5, 0)),))
 
 
 def dg(a, b, ca, cb):
@@ -41,7 +43,7 @@
     gi_ref, gw_ref, gbi_ref, gwo_ref, gbo_ref,
     bin_ref, wo_ref, bout_ref, tgt_ref, vw_ref, xv, wv, act, slope, bp, grad, bcol, ev,
     gp, go, r0, r1, s2, r2, zs, zr, pay, ar0, ar1, ar2, ar3, fin, stage,
-    ld_sem, ev_ss, ev_rs, c_ss, c_rs, s1_ss, s1_rs, s2_ss, s2_rs, z_ss, z_rs,
+    gw_v, gbi_v, gwo_v, gbo_v, ld_sem, ev_ss, ev_rs, c_ss, c_rs, s1_ss, s1_rs, s2_ss, s2_rs, z_ss, z_rs,
     a_ss, a_rs, st_sem,
 ):
     mem = lax.axis_index("member")
@@ -57,6 +59,12 @@
 
     def dz(d):
         return (mem, y * 8 + lax.rem(z + d, 8))
+
+    def dzc(d):
+        return (x * 2 + 1 - c, y * 8 + lax.rem(z + d, 8))
+
+    def dxy(i, j):
+        return (lax.rem(x + i, 4) * 2 + c, lax.rem(y + j, 4) * 8 + z)
 
     partner = (x * 2 + 1 - c, spc)
 
@@ -81,7 +89,7 @@
     for i in range(4):
         part = pl.ds(i * 256, 256)
         wloads.append(pltpu.make_async_copy(w_hbm.at[part, :], wv.at[part, :], ld_sem.at[4 + i]))
-    for k in [xloads[0]] + wloads + xloads[1:]:
+    for k in xloads[:1] + wloads + xloads[1:2]:
         k.start()
     small = [
         pltpu.make_async_copy(src, dst, ld_sem.at[8 + i])
@@ -96,8 +104,10 @@
     for d in range(1, 8):
         pl.semaphore_signal(barrier, inc=1, device_id=(lax.rem(mem + d, 8), spc), device_id_type=MESH)
         pl.semaphore_signal(barrier, inc=1, device_id=dz(d), device_id_type=MESH)
-    for d in range(1, 4):
-        pl.semaphore_signal(barrier, inc=1, device_id=dy(d), device_id_type=MESH)
+        pl.semaphore_signal(barrier, inc=1, device_id=dzc(d), device_id_type=MESH)
+    for i in range(4):
+        for j in range(1, 4):
+            pl.semaphore_signal(barrier, inc=1, device_id=dxy(i, j), device_id_type=MESH)
 
     for k in small:
         k.wait()
@@ -115,6 +125,8 @@
 
     for k in wloads:
         k.wait()
+    for k in xloads[2:]:
+        k.start()
 
     def gather(half, d):
         blk = ev.at[half, mem]
@@ -136,7 +148,7 @@
     for half in range(2):
         lax.fori_loop(2 * half, 2 * half + 2, forward, 0)
         if half == 0:
-            pl.semaphore_wait(barrier, 17)
+            pl.semaphore_wait(barrier, 33)
         for d in range(1, 8):
             cp = gather(half, d)
             cp.start()
@@ -190,12 +202,14 @@
     def cross(s):
         return remote(gp.at[s], r0.at[s], c_ss.at[s], c_rs.at[s], partner)
 
-    def first(s, axis, d):
+    def first(k, d):
+        s, o, w, axis = CHUNKS[k]
+        cols = pl.ds(o, w)
         if axis == 0:
-            src, dev = go.at[s, lax.rem(x + d, 4)], dx(d)
+            src, dev = go.at[s, lax.rem(x + d, 4), :, :, cols], dx(d)
         else:
-            src, dev = go.at[s, :, lax.rem(y + d, 4)], dy(d)
-        return remote(src, r1.at[s, d - 1], s1_ss.at[s, d - 1], s1_rs.at[s, d - 1], dev)
+            src, dev = go.at[s, :, lax.rem(y + d, 4), :, cols], dy(d)
+        return remote(src, r1.at[k, d - 1, :, :, pl.ds(0, w)], s1_ss.at[k, d - 1], s1_rs.at[k, d - 1], dev)
 
     def late(s, carry):
         gp[s] += product(s, 1 - c, 1)
@@ -216,21 +230,26 @@
         pay[q] = jnp.zeros((8, 128), F32)
     a0 = send(pay.at[pl.ds((1 - c) * 8, 8)], ar0, a_ss.at[0], a_rs.at[0], partner)
 
-    def later(p, carry):
-        for axis in range(2):
-            s = 2 * p + axis
-            go[s] += product(s, c, 1)
-            cross(s).wait_recv()
-            go[s] += r0[s]
-            for d in (2, 1, 3):
-                first(s, axis, d).start()
-        return carry
-
-    lax.fori_loop(0, 2, later, 0)
+    s1 = []
+
+    def stage1(s):
+        go[s] += product(s, c, 1)
+        cross(s).wait_recv()
+        go[s] += r0[s]
+
+    def launch(s):
+        for k in range(NCH):
+            if CHUNKS[k][0] == s:
+                s1.append([first(k, d) for d in (2, 1, 3)])
+                for cp in s1[k]:
+                    cp.start()
+                sends.extend(s1[k])
+
+    for s in range(3):
+        stage1(s)
+        launch(s)
+    stage1(3)
     sends += [cross(s) for s in range(4)]
-    s1 = [[first(s, CHUNKS[s], d) for d in (2, 1, 3)] for s in range(4)]
-    for group in s1:
-        sends += group
 
     def out_copy(b):
         r = lax.rem(b, 2) * 512 + (b // 2) * 256
@@ -252,86 +271,106 @@
     a1 = [
         send(ar1.at[lax.rem(z + d, 8)], ar2.at[d - 1], a_ss.at[d], a_rs.at[d], dz(d)) for d in (4, 3, 5, 2, 6, 1, 7)
     ]
-    lax.fori_loop(0, 4, d_block, 0)
+    lax.fori_loop(0, 3, d_block, 0)
     for cp in a1:
         cp.wait_recv()
     ar3[0] = ar1[z] + rsum([ar2[i] for i in range(7)])
-    a2 = [send(ar3.at[0], ar3.at[d], a_ss.at[7 + d], a_rs.at[7 + d], dx(d)) for d in (2, 1, 3)]
-
-    def stage2(s):
-        for cp in s1[s]:
+    a2 = [
+        send(ar3.at[0], ar3.at[4 * i + j], a_ss.at[7 + 4 * i + j], a_rs.at[7 + 4 * i + j], dxy(i, j))
+        for i in range(4)
+        for j in range(4)
+        if i + j > 0
+    ]
+    launch(3)
+    lax.fori_loop(3, 4, d_block, 0)
+
+    def stage2(k):
+        s, o, w, axis = CHUNKS[k]
+        for cp in s1[k]:
             cp.wait_recv()
-        if CHUNKS[s] == 0:
-            s2[s] = go[s, x] + rsum([r1[s, i] for i in range(3)])
-        else:
-            s2[s] = go[s, :, y] + rsum([r1[s, i] for i in range(3)])
+        own = go[s, x, :, :, o : o + w] if axis == 0 else go[s, :, y, :, o : o + w]
+        s2[k, :, :, :w] = own + rsum([r1[k, i, :, :, :w] for i in range(3)])
         out = []
         for d in (2, 1, 3):
-            if CHUNKS[s] == 0:
-                src, dev = s2.at[s, lax.rem(y + d, 4)], dy(d)
+            if axis == 0:
+                src, dev = s2.at[k, lax.rem(y + d, 4), :, pl.ds(0, w)], dy(d)
             else:
-                src, dev = s2.at[s, lax.rem(x + d, 4)], dx(d)
-            out.append(send(src, r2.at[s, d - 1], s2_ss.at[s, d - 1], s2_rs.at[s, d - 1], dev))
+                src, dev = s2.at[k, lax.rem(x + d, 4), :, pl.ds(0, w)], dx(d)
+            out.append(send(src, r2.at[k, d - 1, :, pl.ds(0, w)], s2_ss.at[k, d - 1], s2_rs.at[k, d - 1], dev))
         return out
 
     low = rows8 < 4
 
-    def stage3(pair, e, waits):
-        for j, s in enumerate(pair):
-            for cp in waits[j]:
-                cp.wait_recv()
-            own = y if CHUNKS[s] == 0 else x
-            t = s2[s, own] + rsum([r2[s, i] for i in range(3)])
+    def stage3(e, waits):
+        for j, pair in enumerate(ZGROUPS[e]):
+            half = []
+            for k, o in pair:
+                if o == 0:
+                    for cp in waits[k]:
+                        cp.wait_recv()
+                own = y if CHUNKS[k][3] == 0 else x
+                cols = slice(o, o + 128)
+                half.append(s2[k, own, :, cols] + rsum([r2[k, i, :, cols] for i in range(3)]))
             for p in range(4):
-                u = t[8 * p : 8 * p + 8, :128]
-                v = t[8 * p : 8 * p + 8, 128:]
+                u = half[0][8 * p : 8 * p + 8]
+                v = half[1][8 * p : 8 * p + 8]
                 zs[e, 2 * p, j] = jnp.where(low, u, pltpu.roll(v, 4, 0))
                 zs[e, 2 * p + 1, j] = jnp.where(low, pltpu.roll(u, 4, 0), v)
+        n = pl.ds(0, len(ZGROUPS[e]))
         return [
-            send(zs.at[e, lax.rem(z + d, 8)], zr.at[e, d - 1], z_ss.at[e, d - 1], z_rs.at[e, d - 1], dz(d))
+            send(zs.at[e, lax.rem(z + d, 8), n], zr.at[e, d - 1, n], z_ss.at[e, d - 1], z_rs.at[e, d - 1], dz(d))
             for d in (4, 3, 5, 2, 6, 1, 7)
         ]
 
-    def finish(pair, e, waits):
+    def finish(e, waits):
         for cp in waits:
             cp.wait_recv()
-        for j, s in enumerate(pair):
+        for j, pair in enumerate(ZGROUPS[e]):
             t = zs[e, z, j] + rsum([zr[e, i, j] for i in range(7)])
-            gw_ref[:, s * CW : s * CW + 128] = t[0:4]
-            gw_ref[:, s * CW + 128 : s * CW + 256] = t[4:8]
-
-    w2 = [stage2(s) for s in range(4)]
+            for h, (k, o) in enumerate(pair):
+                c0 = CHUNKS[k][0] * CW + CHUNKS[k][1] + o
+                gw_v[:, c0 : c0 + 128] = t[4 * h : 4 * h + 4]
+
+    w2 = [stage2(k) for k in range(4)]
     for cp in a2:
         cp.wait_recv()
-    ar3[4] = rsum([ar3[i] for i in range(4)])
-    a3 = [send(ar3.at[4], ar3.at[4 + d], a_ss.at[10 + d], a_rs.at[10 + d], dy(d)) for d in (2, 1, 3)]
-    w3a = stage3((0, 1), 0, w2[:2])
-    for cp in a3:
-        cp.wait_recv()
     own = fin.at[c * 8 + z]
-    fin[c * 8 + z] = rsum([ar3[i] for i in range(4, 8)])
-    a4 = [send(own, own, a_ss.at[13 + d], a_rs.at[13 + d], dz(d)) for d in (4, 3, 5, 2, 6, 1, 7)]
-    w3b = stage3((2, 3), 1, w2[2:])
-    finish((0, 1), 0, w3a)
+    fin[c * 8 + z] = rsum([ar3[i] for i in range(16)])
+    a4 = [send(own, own, a_ss.at[22 + d], a_rs.at[22 + d], dz(d)) for d in (4, 3, 5, 2, 6, 1, 7)]
+    a4 += [send(own, own, a_ss.at[30 + d], a_rs.at[30 + d], dzc(d)) for d in (4, 3, 5, 2, 6, 1, 7, 0)]
+    w2 += [stage2(k) for k in range(4, NCH)]
+    w3a = stage3(0, w2)
+    older = list(sends)
+    w3b = stage3(1, w2)
+    finish(0, w3a)
     for cp in a4:
         cp.wait_recv()
-    half_fin = fin.at[pl.ds(c * 8, 8)]
-    a5 = send(half_fin, half_fin, a_ss.at[21], a_rs.at[21], partner)
-    a5.wait_recv()
     for q in range(8):
-        gwo_ref[:, q * 128 : (q + 1) * 128] = fin[q]
+        gwo_v[:, q * 128 : (q + 1) * 128] = fin[q]
     bo = jnp.sum(fin[8], axis=1, keepdims=True)
     for v in range(8):
-        gbo_ref[v] = jnp.sum(jnp.where(rows8[:, :1] == v, bo, 0.0))
+        gbo_v[v] = jnp.sum(jnp.where(rows8[:, :1] == v, bo, 0.0))
     lanes = lax.broadcasted_iota(jnp.int32, (8, 128), 1)
     bi = fin[9]
     for r in range(4):
-        gbi_ref[r] = jnp.sum(jnp.where((rows8 == mem) & (lanes == spc * 4 + r), bi, 0.0))
-    finish((2, 3), 1, w3b)
-    for cp in sends:
+        gbi_v[r] = jnp.sum(jnp.where((rows8 == mem) & (lanes == spc * 4 + r), bi, 0.0))
+    results = [
+        pltpu.make_async_copy(src, dst, st_sem.at[4 + i])
+        for i, (src, dst) in enumerate(((gwo_v, gwo_ref), (gbo_v, gbo_ref), (gbi_v, gbi_ref)))
+    ]
+    for cp in results:
+        cp.start()
+    for cp in older:
         cp.wait_send()
     for b in range(4):
         out_copy(b).wait()
+    finish(1, w3b)
+    last = pltpu.make_async_copy(gw_v, gw_ref, st_sem.at[7])
+    last.start()
+    for cp in w3b:
+        cp.wait_send()
+    for cp in results + [last]:
+        cp.wait()
 
 
 def place(*refs):
@@ -351,8 +390,6 @@
 
 def shards(inputs, weight_in, bias_in, weight_out, bias_out, target_field, variable_weight):
     rows = inputs.reshape(1024, 1024)
-    vm = pl.BlockSpec(memory_space=pltpu.VMEM)
-    sm = pl.BlockSpec(memory_space=pltpu.SMEM)
     hb = pl.BlockSpec(memory_space=pl.ANY)
     dma = pltpu.SemaphoreType.DMA
     gi, gw, gbi, gwo, gbo = pl.pallas_call(
@@ -365,7 +402,7 @@
             jax.ShapeDtypeStruct((8,), F32),
         ),
         in_specs=[hb, hb, hb, hb, hb, hb, hb],
-        out_specs=(hb, vm, sm, vm, sm),
+        out_specs=(hb,) * 5,
         scratch_shapes=[
             pltpu.VMEM((1, 1024), F32),
             pltpu.VMEM((8, 1024), BF),
@@ -383,26 +420,30 @@
             pltpu.VMEM((4, 4, 4, 32, CW), F32),
             pltpu.VMEM((4, 4, 4, 32, CW), F32),
             pltpu.VMEM((4, 4, 4, 32, CW), F32),
-            pltpu.VMEM((4, 3, 4, 32, CW), F32),
-            pltpu.VMEM((4, 4, 32, CW), F32),
-            pltpu.VMEM((4, 3, 32, CW), F32),
-            pltpu.VMEM((2, 8, 2, 8, 128), F32),
-            pltpu.VMEM((2, 7, 2, 8, 128), F32),
+            pltpu.VMEM((NCH, 3, 4, 32, CW), F32),
+            pltpu.VMEM((NCH, 4, 32, CW), F32),
+            pltpu.VMEM((NCH, 3, 32, CW), F32),
+            pltpu.VMEM((2, 8, 3, 8, 128), F32),
+            pltpu.VMEM((2, 7, 3, 8, 128), F32),
             pltpu.VMEM((16, 8, 128), F32),
             pltpu.VMEM((8, 8, 128), F32),
             pltpu.VMEM((8, 8, 128), F32),
             pltpu.VMEM((7, 8, 128), F32),
-            pltpu.VMEM((8, 8, 128), F32),
+            pltpu.VMEM((16, 8, 128), F32),
             pltpu.VMEM((16, 8, 128), F32),
             pltpu.VMEM((1024, 1024), BF),
+            pltpu.VMEM((4, 1024), F32),
+            pltpu.SMEM((4,), F32),
+            pltpu.VMEM((8, 1024), F32),
+            pltpu.SMEM((8,), F32),
             dma((13,)),
             dma((2, 7)), dma((2, 7)),
             dma((4,)), dma((4,)),
-            dma((4, 3)), dma((4, 3)),
-            dma((4, 3)), dma((4, 3)),
+            dma((NCH, 3)), dma((NCH, 3)),
+            dma((NCH, 3)), dma((NCH, 3)),
             dma((2, 7)), dma((2, 7)),
-            dma((22,)), dma((22,)),
-            dma((4,)),
+            dma((38,)), dma((38,)),
+            dma((8,)),
         ],
         compiler_params=pltpu.CompilerParams(
             collective_id=0, has_side_effects=True, vmem_limit_bytes=60 * 2**20

time: 51.8 us -> 48.8 us (0.942)
  the two profiles are of different devices: /device:TPU:1 before, /device:TPU:2 now
where the time goes in v3:
time: 48.8 us; the launch traced here: 48.7 us
  Pallas kernels  48.1 us (99%)
  between operations  0.64 us (1%)
    pallas_call x1, Pallas kernels, shards(): pl.pallas_call(kernel, out_shape=(jax.ShapeDtypeStruct((1024, 1024), BF),...  45.6 us
    pallas_call x1, Pallas kernels, shards(): pl.pallas_call(place, out_shape=tuple((jax.ShapeDtypeStruct(a.shape, a.dt...  2.48 us

profile of v3, /device:TPU:2, one launch (start us, length us, event | category | flops | bytes accessed | tf_op | source)
XLA Modules:
  0.0 48.7 jit_solution(9095099448177119797)
XLA Ops:
  0.6 45.6 %crps_backward.1 = (bf16[1024,1024]{1,0:T(8,128)(2,1)}, f32[4,1024]{1,0:T(4,128)}, f32[4]{0:T(128)}, f32[8,1024]{1,0:T(8,128)}, f32[8]{0:T(128)}) custom-call(bf16[1024,1024]{1,0:T(8,128)(2,1)} %bitcast.3, bf16[1024,1024]{1,0:T(8,128)(2,1)} %w_hbm.1, f32[1,1024]{1,0:T(1,128)} %bitcast.5, bf16[8,1024]{1,0:T(8,128)(2,1)} %wo_hbm.1, f32[8]{0:T(128)} %bout_hbm.1, ...), custom_call_target="tpu_custom_call" | custom-call | flops 6442450944 | bytes 7340032 | tf_op jit(solution)/shard_map/crps_backward/pallas_call | solution.py:395
  46.2 2.5 %place.1 = (bf16[1024,1024]{1,0:T(8,128)(2,1)}, f32[4,1024]{1,0:T(4,128)}, f32[4]{0:T(128)}, f32[8,1024]{1,0:T(8,128)}, f32[8]{0:T(128)}) custom-call(bf16[1024,1024]{1,0:T(8,128)(2,1)} %get-tuple-element.15.refs_0_, f32[4,1024]{1,0:T(4,128)} %get-tuple-element.16.refs_1_, f32[4]{0:T(128)} %get-tuple-element.17.refs_2_, ...), custom_call_target="tpu_custom_call" | custom-call | tf_op jit(solution)/shard_map/place/pallas_call | solution.py:454

commit v4 on v3

--- a/solution.py
+++ b/solution.py
@@ -24,7 +24,8 @@
 CW = 256
 CHUNKS = ((0, 0, 128, 0), (0, 128, 128, 1), (1, 0, 256, 0), (2, 0, 256, 1), (3, 0, 128, 0), (3, 128, 128, 1))
 NCH = len(CHUNKS)
-ZGROUPS = ((((0, 0), (1, 0)), ((2, 0), (2, 128)), ((3, 0), (3, 128))), (((4, 0), (5, 0)),))
+RELAYED = 4
+ZGROUPS = ((((4, 0), (5, 0)), ((0, 0), (1, 0))), (((2, 0), (2, 128)), ((3, 0), (3, 128))))
 
 
 def dg(a, b, ca, cb):
@@ -42,8 +43,8 @@
     x_hbm, w_hbm, bin_hbm, wo_hbm, bout_hbm, tgt_hbm, vw_hbm,
     gi_ref, gw_ref, gbi_ref, gwo_ref, gbo_ref,
     bin_ref, wo_ref, bout_ref, tgt_ref, vw_ref, xv, wv, act, slope, bp, grad, bcol, ev,
-    gp, go, r0, r1, s2, r2, zs, zr, pay, ar0, ar1, ar2, ar3, fin, stage,
-    gw_v, gbi_v, gwo_v, gbo_v, ld_sem, ev_ss, ev_rs, c_ss, c_rs, s1_ss, s1_rs, s2_ss, s2_rs, z_ss, z_rs,
+    gp, go, r0, r1, rl, s2, r2, zs, zr, pay, ar0, ar1, ar2, ar3, fin, stage,
+    gw_v, gbi_v, gwo_v, gbo_v, ld_sem, ev_ss, ev_rs, c_ss, c_rs, rl_ss, rl_rs, s1_ss, s1_rs, s2_ss, s2_rs, z_ss, z_rs,
     a_ss, a_rs, st_sem,
 ):
     mem = lax.axis_index("member")
@@ -202,6 +203,11 @@
     def cross(s):
         return remote(gp.at[s], r0.at[s], c_ss.at[s], c_rs.at[s], partner)
 
+    def cross_part(o):
+        cols = pl.ds(o, 128)
+        i = 4 * (o // 128)
+        return remote(gp.at[0, :, :, :, cols], r0.at[0, :, :, :, cols], c_ss.at[i], c_rs.at[i], partner)
+
     def first(k, d):
         s, o, w, axis = CHUNKS[k]
         cols = pl.ds(o, w)
@@ -209,14 +215,68 @@
             src, dev = go.at[s, lax.rem(x + d, 4), :, :, cols], dx(d)
         else:
             src, dev = go.at[s, :, lax.rem(y + d, 4), :, cols], dy(d)
-        return remote(src, r1.at[k, d - 1, :, :, pl.ds(0, w)], s1_ss.at[k, d - 1], s1_rs.at[k, d - 1], dev)
+        i = k - RELAYED
+        return remote(src, r1.at[i, d - 1, :, :, pl.ds(0, w)], s1_ss.at[i, d - 1], s1_rs.at[i, d - 1], dev)
+
+    MESSAGES = ((1, 1, 1), (2, 0, 1), (3, 0, 3), (2, 1, 3), (1, 0, 1), (3, 1, 3))
+
+    def place_of(k, j, h):
+        s, o, w, axis = CHUNKS[k]
+        if axis == 0:
+            return (s, lax.rem(x + j, 4), pl.ds(2 * h, 2), slice(None), pl.ds(o, w))
+        return (s, pl.ds(2 * h, 2), lax.rem(y + j, 4), slice(None), pl.ds(o, w))
+
+    def message(k, slot):
+        j, h, d = MESSAGES[slot]
+        w, axis = CHUNKS[k][2:]
+        dst = rl.at[k, slot, :, :, pl.ds(0, w)]
+        return remote(go.at[place_of(k, j, h)], dst, rl_ss.at[k, slot], rl_rs.at[k, slot], dx(d) if axis == 0 else dy(d))
 
     def late(s, carry):
         gp[s] += product(s, 1 - c, 1)
         cross(s).start()
         return carry
 
-    lax.fori_loop(0, 4, late, 0)
+    gp[0] += product(0, 1 - c, 1)
+    crossed = [cross_part(0), cross_part(128)]
+    for cp in crossed:
+        cp.start()
+    lax.fori_loop(1, 4, late, 0)
+    crossed += [cross(s) for s in range(1, 4)]
+
+    def own_product(s, carry):
+        go[s] += product(s, c, 1)
+        return carry
+
+    lax.fori_loop(0, 3, own_product, 0)
+
+    s1 = []
+
+    def launch(k):
+        if k < RELAYED:
+            group = [message(k, slot) for slot in (1, 3, 0, 2)]
+        else:
+            group = [first(k, d) for d in (2, 1, 3)]
+        s1.append(group)
+        for cp in group:
+            cp.start()
+        sends.extend(group)
+
+    def relay(k):
+        w = CHUNKS[k][2]
+        for slot in (1, 3):
+            s1[k][slot // 2].wait_recv()
+            at = place_of(k, *MESSAGES[slot // 2 + 4][:2])
+            go[at] += rl[k, slot, :, :, :w]
+            cp = message(k, slot // 2 + 4)
+            cp.start()
+            s1[k].append(cp)
+            sends.append(cp)
+
+    for k, o in enumerate((0, 128)):
+        crossed[k].wait_recv()
+        go[0, :, :, :, o : o + 128] += r0[0, :, :, :, o : o + 128]
+        launch(k)
 
     for q in range(0, 1024, 256):
         t = dg(grad[...].astype(BF), act[:, q : q + 256], 1, 0)
@@ -230,26 +290,14 @@
         pay[q] = jnp.zeros((8, 128), F32)
     a0 = send(pay.at[pl.ds((1 - c) * 8, 8)], ar0, a_ss.at[0], a_rs.at[0], partner)
 
-    s1 = []
-
-    def stage1(s):
-        go[s] += product(s, c, 1)
-        cross(s).wait_recv()
+    for s in (1, 2):
+        crossed[s + 1].wait_recv()
         go[s] += r0[s]
-
-    def launch(s):
-        for k in range(NCH):
-            if CHUNKS[k][0] == s:
-                s1.append([first(k, d) for d in (2, 1, 3)])
-                for cp in s1[k]:
-                    cp.start()
-                sends.extend(s1[k])
-
-    for s in range(3):
-        stage1(s)
-        launch(s)
-    stage1(3)
-    sends += [cross(s) for s in range(4)]
+        launch(s + 1)
+    go[3] += product(3, c, 1)
+    crossed[4].wait_recv()
+    go[3] += r0[3]
+    sends += crossed
 
     def out_copy(b):
         r = lax.rem(b, 2) * 512 + (b // 2) * 256
@@ -271,7 +319,14 @@
     a1 = [
         send(ar1.at[lax.rem(z + d, 8)], ar2.at[d - 1], a_ss.at[d], a_rs.at[d], dz(d)) for d in (4, 3, 5, 2, 6, 1, 7)
     ]
-    lax.fori_loop(0, 3, d_block, 0)
+    launch(4)
+    launch(5)
+    lax.fori_loop(0, 1, d_block, 0)
+    relay(0)
+    relay(1)
+    lax.fori_loop(1, 3, d_block, 0)
+    relay(2)
+    relay(3)
     for cp in a1:
         cp.wait_recv()
     ar3[0] = ar1[z] + rsum([ar2[i] for i in range(7)])
@@ -281,15 +336,18 @@
         for j in range(4)
         if i + j > 0
     ]
-    launch(3)
     lax.fori_loop(3, 4, d_block, 0)
 
     def stage2(k):
         s, o, w, axis = CHUNKS[k]
-        for cp in s1[k]:
+        for cp in s1[k][2:] if k < RELAYED else s1[k]:
             cp.wait_recv()
         own = go[s, x, :, :, o : o + w] if axis == 0 else go[s, :, y, :, o : o + w]
-        s2[k, :, :, :w] = own + rsum([r1[k, i, :, :, :w] for i in range(3)])
+        if k < RELAYED:
+            s2[k, 0:2, :, :w] = own[0:2] + rl[k, 2, :, :, :w] + rl[k, 4, :, :, :w]
+            s2[k, 2:4, :, :w] = own[2:4] + rl[k, 0, :, :, :w] + rl[k, 5, :, :, :w]
+        else:
+            s2[k, :, :, :w] = own + rsum([r1[k - RELAYED, i, :, :, :w] for i in range(3)])
         out = []
         for d in (2, 1, 3):
             if axis == 0:
@@ -331,14 +389,13 @@
                 c0 = CHUNKS[k][0] * CW + CHUNKS[k][1] + o
                 gw_v[:, c0 : c0 + 128] = t[4 * h : 4 * h + 4]
 
-    w2 = [stage2(k) for k in range(4)]
+    w2 = {k: stage2(k) for k in (4, 5, 0, 1, 2, 3)}
     for cp in a2:
         cp.wait_recv()
     own = fin.at[c * 8 + z]
     fin[c * 8 + z] = rsum([ar3[i] for i in range(16)])
     a4 = [send(own, own, a_ss.at[22 + d], a_rs.at[22 + d], dz(d)) for d in (4, 3, 5, 2, 6, 1, 7)]
     a4 += [send(own, own, a_ss.at[30 + d], a_rs.at[30 + d], dzc(d)) for d in (4, 3, 5, 2, 6, 1, 7, 0)]
-    w2 += [stage2(k) for k in range(4, NCH)]
     w3a = stage3(0, w2)
     older = list(sends)
     w3b = stage3(1, w2)
@@ -420,11 +477,12 @@
             pltpu.VMEM((4, 4, 4, 32, CW), F32),
             pltpu.VMEM((4, 4, 4, 32, CW), F32),
             pltpu.VMEM((4, 4, 4, 32, CW), F32),
-            pltpu.VMEM((NCH, 3, 4, 32, CW), F32),
+            pltpu.VMEM((NCH - RELAYED, 3, 4, 32, 128), F32),
+            pltpu.VMEM((RELAYED, 6, 2, 32, CW), F32),
             pltpu.VMEM((NCH, 4, 32, CW), F32),
             pltpu.VMEM((NCH, 3, 32, CW), F32),
-            pltpu.VMEM((2, 8, 3, 8, 128), F32),
-            pltpu.VMEM((2, 7, 3, 8, 128), F32),
+            pltpu.VMEM((2, 8, 2, 8, 128), F32),
+            pltpu.VMEM((2, 7, 2, 8, 128), F32),
             pltpu.VMEM((16, 8, 128), F32),
             pltpu.VMEM((8, 8, 128), F32),
             pltpu.VMEM((8, 8, 128), F32),
@@ -438,7 +496,8 @@
             pltpu.SMEM((8,), F32),
             dma((13,)),
             dma((2, 7)), dma((2, 7)),
-            dma((4,)), dma((4,)),
+            dma((5,)), dma((5,)),
+            dma((RELAYED, 6)), dma((RELAYED, 6)),
             dma((NCH, 3)), dma((NCH, 3)),
             dma((NCH, 3)), dma((NCH, 3)),
             dma((2, 7)), dma((2, 7)),

time: 48.8 us -> 47.9 us (0.982)
  Pallas kernels: 48.1 us -> 47.1 us
    pallas_call x1, Pallas kernels: 45.6 us -> 44.6 us  [shards(): pl.pallas_call(kernel, out_shape=(jax.ShapeDtypeStruct((1024, 1024), BF),...]
where the time goes in v4:
time: 47.9 us; the launch traced here: 47.7 us
  Pallas kernels  47.1 us (98%)
  between operations  0.64 us (1%)
    pallas_call x1, Pallas kernels, shards(): pl.pallas_call(kernel, out_shape=(jax.ShapeDtypeStruct((1024, 1024), BF),...  44.6 us
    pallas_call x1, Pallas kernels, shards(): pl.pallas_call(place, out_shape=tuple((jax.ShapeDtypeStruct(a.shape, a.dt...  2.48 us

profile of v4, /device:TPU:2, one launch (start us, length us, event | category | flops | bytes accessed | tf_op | source)
XLA Modules:
  0.0 47.7 jit_solution(11392416263796533435)
XLA Ops:
  0.6 44.6 %crps_backward.1 = (bf16[1024,1024]{1,0:T(8,128)(2,1)}, f32[4,1024]{1,0:T(4,128)}, f32[4]{0:T(128)}, f32[8,1024]{1,0:T(8,128)}, f32[8]{0:T(128)}) custom-call(bf16[1024,1024]{1,0:T(8,128)(2,1)} %bitcast.3, bf16[1024,1024]{1,0:T(8,128)(2,1)} %w_hbm.1, f32[1,1024]{1,0:T(1,128)} %bitcast.5, bf16[8,1024]{1,0:T(8,128)(2,1)} %wo_hbm.1, f32[8]{0:T(128)} %bout_hbm.1, ...), custom_call_target="tpu_custom_call" | custom-call | flops 6442450944 | bytes 7340032 | tf_op jit(solution)/shard_map/crps_backward/pallas_call | solution.py:452
  45.2 2.5 %place.1 = (bf16[1024,1024]{1,0:T(8,128)(2,1)}, f32[4,1024]{1,0:T(4,128)}, f32[4]{0:T(128)}, f32[8,1024]{1,0:T(8,128)}, f32[8]{0:T(128)}) custom-call(bf16[1024,1024]{1,0:T(8,128)(2,1)} %get-tuple-element.15.refs_0_, f32[4,1024]{1,0:T(4,128)} %get-tuple-element.16.refs_1_, f32[4]{0:T(128)} %get-tuple-element.17.refs_2_, ...), custom_call_target="tpu_custom_call" | custom-call | tf_op jit(solution)/shard_map/place/pallas_call | solution.py:513

commit v5 on v4

--- a/solution.py
+++ b/solution.py
@@ -331,11 +331,18 @@
         cp.wait_recv()
     ar3[0] = ar1[z] + rsum([ar2[i] for i in range(7)])
     a2 = [
-        send(ar3.at[0], ar3.at[4 * i + j], a_ss.at[7 + 4 * i + j], a_rs.at[7 + 4 * i + j], dxy(i, j))
+        remote(ar3.at[0], ar3.at[4 * i + j], a_ss.at[7 + 4 * i + j], a_rs.at[7 + 4 * i + j], dxy(i, j))
         for i in range(4)
         for j in range(4)
         if i + j > 0
     ]
+    used = jnp.logical_or(c == 0, z < 2)
+
+    @pl.when(used)
+    def _():
+        for cp in a2:
+            cp.start()
+
     lax.fori_loop(3, 4, d_block, 0)
 
     def stage2(k):
@@ -390,10 +397,13 @@
                 gw_v[:, c0 : c0 + 128] = t[4 * h : 4 * h + 4]
 
     w2 = {k: stage2(k) for k in (4, 5, 0, 1, 2, 3)}
-    for cp in a2:
-        cp.wait_recv()
+    @pl.when(used)
+    def _():
+        for cp in a2:
+            cp.wait()
+
     own = fin.at[c * 8 + z]
-    fin[c * 8 + z] = rsum([ar3[i] for i in range(16)])
+    fin[c * 8 + z] = jnp.where(used, rsum([ar3[i] for i in range(16)]), 0.0)
     a4 = [send(own, own, a_ss.at[22 + d], a_rs.at[22 + d], dz(d)) for d in (4, 3, 5, 2, 6, 1, 7)]
     a4 += [send(own, own, a_ss.at[30 + d], a_rs.at[30 + d], dzc(d)) for d in (4, 3, 5, 2, 6, 1, 7, 0)]
     w3a = stage3(0, w2)

time: 47.9 us -> 47.6 us (level)
  no operation moved by 1% of the time
where the time goes in v5:
time: 47.6 us; the launch traced here: 47.5 us
  Pallas kernels  46.8 us (98%)
  between operations  0.64 us (1%)
    pallas_call x1, Pallas kernels, shards(): pl.pallas_call(kernel, out_shape=(jax.ShapeDtypeStruct((1024, 1024), BF),...  44.3 us
    pallas_call x1, Pallas kernels, shards(): pl.pallas_call(place, out_shape=tuple((jax.ShapeDtypeStruct(a.shape, a.dt...  2.48 us

profile of v5, /device:TPU:2, one launch (start us, length us, event | category | flops | bytes accessed | tf_op | source)
XLA Modules:
  0.0 47.5 jit_solution(5080179818713036325)
XLA Ops:
  0.6 44.3 %crps_backward.1 = (bf16[1024,1024]{1,0:T(8,128)(2,1)}, f32[4,1024]{1,0:T(4,128)}, f32[4]{0:T(128)}, f32[8,1024]{1,0:T(8,128)}, f32[8]{0:T(128)}) custom-call(bf16[1024,1024]{1,0:T(8,128)(2,1)} %bitcast.3, bf16[1024,1024]{1,0:T(8,128)(2,1)} %w_hbm.1, f32[1,1024]{1,0:T(1,128)} %bitcast.5, bf16[8,1024]{1,0:T(8,128)(2,1)} %wo_hbm.1, f32[8]{0:T(128)} %bout_hbm.1, ...), custom_call_target="tpu_custom_call" | custom-call | flops 6442450944 | bytes 7340032 | tf_op jit(solution)/shard_map/crps_backward/pallas_call | solution.py:462
  45.0 2.5 %place.1 = (bf16[1024,1024]{1,0:T(8,128)(2,1)}, f32[4,1024]{1,0:T(4,128)}, f32[4]{0:T(128)}, f32[8,1024]{1,0:T(8,128)}, f32[8]{0:T(128)}) custom-call(bf16[1024,1024]{1,0:T(8,128)(2,1)} %get-tuple-element.15.refs_0_, f32[4,1024]{1,0:T(4,128)} %get-tuple-element.16.refs_1_, f32[4]{0:T(128)} %get-tuple-element.17.refs_2_, ...), custom_call_target="tpu_custom_call" | custom-call | tf_op jit(solution)/shard_map/place/pallas_call | solution.py:523
